TPU v7x, 32 devices: a whole 2x2x4 slice. The times are simulated.
32 devices in a mesh: groups: 2 (over y), wide: 8 (over z, x), narrow: 2 (over core).
Axes of the slice: x: 2, y: 2, z: 4, core: 2. Of those that a mesh axis runs over, the one named last changes fastest.
Arguments:
- inputs: bfloat16 [8192, 1024], P(('groups', 'wide', 'narrow')), parts along dimension 0, may hold values from -6 to 6
- filter_taps: bfloat16 [4096, 1024], P(('wide', 'narrow')), may hold values from -6 to 6
- grad_out: bfloat16 [8192, 1024], P(('groups', 'wide', 'narrow')), parts along dimension 0, may hold values from -6 to 6
Outputs:
- outputs: bfloat16 [8192, 1024], P(('groups', 'wide', 'narrow')), parts along dimension 0
- grad_inputs: bfloat16 [8192, 1024], P(('groups', 'wide', 'narrow')), parts along dimension 0
- grad_taps: bfloat16 [8192, 1024], P(('groups', 'wide', 'narrow')), parts along dimension 0
There are 2 independent parts, one for each index of `groups`. A program takes and returns all parts, laid end to end along the dimension named above; an argument that names none is the same for every part. Nothing has to cross between parts.
All inputs are finite; a program needn't handle non-finite values.
Results may differ from a plain program's by a relative error of at most 0.008.
Values may be sent and summed in bfloat16 or wider, within the bound.
A program may use at most 64 MiB of HBM per device.

v0:
```python
import math

import jax
import jax.numpy as jnp
from jax import lax
from jax.sharding import PartitionSpec as P


def partner_2(value, axis, distance):
    mask = 2**distance
    pairs = [(source, source ^ mask) for source in range(lax.axis_size(axis))]
    return lax.ppermute(value, axis, pairs)


def on_device(inputs, filter_taps, grad_out):
    span_count = lax.axis_size("wide")
    blocksize = inputs.shape[0]
    channels = inputs.shape[1]
    shares = channels // span_count
    row_count = span_count * shares
    seq_len = span_count * 2 * blocksize
    parity = lax.axis_index("narrow")
    signed = (1 - 2 * parity).astype(jnp.float32)
    counter = jnp.arange(span_count, dtype=jnp.int32)
    long_angles = (counter[:, None] * counter[None, :] % span_count).astype(jnp.float32) * (
        2.0 * math.pi / span_count
    )
    long_cos = jnp.cos(long_angles)
    long_sin = jnp.sin(long_angles)
    long_forward = jnp.concatenate([long_cos, -long_sin], axis=0).astype(jnp.bfloat16)
    long_inverse = jnp.concatenate([long_cos, -long_sin], axis=1).astype(jnp.bfloat16)
    positions = jnp.arange(blocksize, dtype=jnp.int32)

    def first_section(pieces, twist_cos, twist_sin):
        share_count = pieces.shape[1]
        lane_count = pieces.shape[2]
        flatten = pieces.reshape(span_count, share_count * lane_count)
        mixture = jnp.dot(long_forward, flatten, preferred_element_type=jnp.float32)
        mixture = mixture.reshape(2, span_count, share_count, lane_count)
        real_part = mixture[0] * twist_cos + mixture[1] * twist_sin
        imag_part = mixture[1] * twist_cos - mixture[0] * twist_sin
        return jnp.stack([real_part, imag_part]).astype(jnp.bfloat16)

    def long_back(combined_re, combined_im, twist_cos, twist_sin):
        merged_re = combined_re * twist_cos - combined_im * twist_sin
        merged_im = combined_im * twist_cos + combined_re * twist_sin
        share_count = combined_re.shape[1]
        lane_count = combined_re.shape[2]
        stacked = (
            jnp.stack([merged_re, merged_im])
            .astype(jnp.bfloat16)
            .reshape(2 * span_count, share_count * lane_count)
        )
        summed = jnp.dot(long_inverse, stacked, preferred_element_type=jnp.float32) * (
            1.0 / seq_len
        )
        return summed.astype(jnp.bfloat16).reshape(span_count, share_count, lane_count)

    block_product = positions[:, None] * (2 * positions[None, :] + parity) % (2 * blocksize)
    block_angles = block_product.astype(jnp.float32) * (math.pi / blocksize)
    block_cos = jnp.cos(block_angles)
    block_sin = jnp.sin(block_angles)
    forward_mat = jnp.concatenate(
        [
            jnp.concatenate([block_cos, -block_sin], axis=1),
            jnp.concatenate([block_sin, block_cos], axis=1),
        ],
        axis=0,
    ).astype(jnp.bfloat16)
    cos_turned = jnp.transpose(block_cos)
    sin_turned = jnp.transpose(block_sin)
    inverse_mat = jnp.concatenate(
        [
            jnp.concatenate([cos_turned, sin_turned], axis=1),
            jnp.concatenate([-sin_turned, cos_turned], axis=1),
        ],
        axis=0,
    ).astype(jnp.bfloat16)
    twist_product = (parity * blocksize + positions)[None, None, :] * counter[:, None, None]
    twist_angles = twist_product.astype(jnp.float32) * (2.0 * math.pi / seq_len)
    twist_cos = jnp.cos(twist_angles)
    twist_sin = jnp.sin(twist_angles)

    def section_pairs(pieces):
        return first_section(pieces, twist_cos, twist_sin)

    def spectrum(signal):
        arranged = jnp.transpose(signal).reshape(span_count, shares, blocksize)
        twisted = section_pairs(
            lax.all_to_all(arranged, "wide", split_axis=0, concat_axis=0, tiled=True)
        )
        partner = partner_2(twisted, "narrow", 0)
        paired = (signed * twisted.astype(jnp.float32) + partner.astype(jnp.float32)).astype(
            jnp.bfloat16
        )
        joined = jnp.concatenate(
            [paired[0].reshape(row_count, blocksize), paired[1].reshape(row_count, blocksize)],
            axis=1,
        )
        return jnp.dot(joined, forward_mat, preferred_element_type=jnp.float32)

    def invert(spectrum_in):
        unfolded = jnp.dot(spectrum_in, inverse_mat, preferred_element_type=jnp.float32).astype(
            jnp.bfloat16
        )
        partner = partner_2(unfolded, "narrow", 0)
        combined = signed * unfolded.astype(jnp.float32) + partner.astype(jnp.float32)
        comb_re = combined[:, :blocksize].reshape(span_count, shares, blocksize)
        comb_im = combined[:, blocksize:].reshape(span_count, shares, blocksize)
        arranged = long_back(comb_re, comb_im, twist_cos, twist_sin)
        returned = lax.all_to_all(arranged, "wide", split_axis=0, concat_axis=1, tiled=True)
        return jnp.transpose(returned.reshape(channels, blocksize))

    def product(left_side, right_side, conjugate, factor):
        left_re = left_side[..., :blocksize]
        left_im = left_side[..., blocksize:]
        right_re = right_side[..., :blocksize]
        right_im = right_side[..., blocksize:]
        if conjugate:
            real_part = left_re * right_re + left_im * right_im
            imag_part = left_re * right_im - left_im * right_re
        else:
            real_part = left_re * right_re - left_im * right_im
            imag_part = left_re * right_im + left_im * right_re
        return (jnp.concatenate([real_part, imag_part], axis=-1) * factor).astype(jnp.bfloat16)

    kernel_scale = 1.0 / math.sqrt(seq_len)
    input_spectrum = spectrum(inputs)
    kernel_spectrum = spectrum(filter_taps) * kernel_scale
    outputs = invert(product(kernel_spectrum, input_spectrum, False, 1.0))
    grad_spectrum = spectrum(grad_out)
    grad_inputs = invert(product(kernel_spectrum, grad_spectrum, True, 1.0))
    grad_taps = invert(product(input_spectrum, grad_spectrum, True, kernel_scale))
    return (outputs, grad_inputs, grad_taps)


def solution(mesh):
    in_specs = (
        P(("groups", "wide", "narrow"), None),
        P(("wide", "narrow"), None),
        P(("groups", "wide", "narrow"), None),
    )
    out_specs = (
        P(("groups", "wide", "narrow"), None),
        P(("groups", "wide", "narrow"), None),
        P(("groups", "wide", "narrow"), None),
    )
    return jax.shard_map(
        on_device, mesh=mesh, in_specs=in_specs, out_specs=out_specs, check_vma=False
    )
```

profile of v0, /device:TPU:0, one launch (start us, length us, event | category | flops | bytes accessed | tf_op | source)
XLA Modules:
  0.0 144.9 jit_solution(16948435035127631216)
XLA Ops:
  0.7 2.1 %copy.61 = bf16[1024,256]{1,0:T(8,128)(2,1)} copy(bf16[1024,256]{0,1:T(8,128)(2,1)} %bitcast.84) | data formatting | bytes 1048576 | tf_op jit(solution)/shard_map/reshape | solution.py:88
  2.8 7.3 %all-to-all-start.1 = ((bf16[8,128,256]{2,1,0:T(8,128)(2,1)}), bf16[8,128,256]{2,1,0:T(8,128)(2,1)S(1)}, u32[]{:S(2)}, u32[]{:S(2)}) async-start(bf16[8,128,256]{2,1,0:T(8,128)(2,1)} %bitcast.7), calls=%async_computation.1 | async-start | bytes 1048576 | tf_op jit(solution)/shard_map/all_to_all | solution.py:90
  10.0 1.0 copy.60
  11.0 13.5 %all-to-all-done.1 = bf16[8,128,256]{2,1,0:T(8,128)(2,1)S(1)} async-done(((bf16[8,128,256]{2,1,0:T(8,128)(2,1)}), bf16[8,128,256]{2,1,0:T(8,128)(2,1)S(1)}, u32[]{:S(2)}, u32[]{:S(2)}) %all-to-all-start.1) | async-done | bytes 524320 | tf_op jit(solution)/shard_map/all_to_all | solution.py:90
  24.5 3.6 %all-to-all-start = ((bf16[8,128,256]{2,1,0:T(8,128)(2,1)}), bf16[8,128,256]{2,1,0:T(8,128)(2,1)S(1)}, u32[]{:S(2)}, u32[]{:S(2)}) async-start(bf16[8,128,256]{2,1,0:T(8,128)(2,1)} %bitcast.1), calls=%async_computation | async-start | bytes 1048576 | tf_op jit(solution)/shard_map/all_to_all | solution.py:90
  28.2 1.0 copy.62
  29.2 13.7 %all-to-all-done = bf16[8,128,256]{2,1,0:T(8,128)(2,1)S(1)} async-done(((bf16[8,128,256]{2,1,0:T(8,128)(2,1)}), bf16[8,128,256]{2,1,0:T(8,128)(2,1)S(1)}, u32[]{:S(2)}, u32[]{:S(2)}) %all-to-all-start) | async-done | bytes 524320 | tf_op jit(solution)/shard_map/all_to_all | solution.py:90
  42.8 3.6 %all-to-all-start.3 = ((bf16[8,128,256]{2,1,0:T(8,128)(2,1)}), bf16[8,128,256]{2,1,0:T(8,128)(2,1)S(1)}, u32[]{:S(2)}, u32[]{:S(2)}) async-start(bf16[8,128,256]{2,1,0:T(8,128)(2,1)} %bitcast.18), calls=%async_computation.3 | async-start | bytes 1048576 | tf_op jit(solution)/shard_map/all_to_all | solution.py:90
  46.6 0.3 copy.64
  46.9 0.3 copy.63
  47.2 13.9 %all-to-all-done.3 = bf16[8,128,256]{2,1,0:T(8,128)(2,1)S(1)} async-done(((bf16[8,128,256]{2,1,0:T(8,128)(2,1)}), bf16[8,128,256]{2,1,0:T(8,128)(2,1)S(1)}, u32[]{:S(2)}, u32[]{:S(2)}) %all-to-all-start.3) | async-done | bytes 524320 | tf_op jit(solution)/shard_map/all_to_all | solution.py:90
  61.1 0.3 copy.66
  61.4 0.4 fusion.47
  61.8 0.1 fusion.62
  62.0 0.4 fusion.49
  62.4 0.1 fusion.64
  62.5 0.4 fusion.48
  63.0 0.1 fusion.65
  63.1 2.8 %add_convert_fusion.6 = (bf16[1,8,128,256]{3,2,1,0:T(8,128)(2,1)S(1)}, bf16[1,8,128,256]{3,2,1,0:T(8,128)(2,1)S(1)}, bf16[1,8,128,256]{3,2,1,0:T(8,128)(2,1)S(1)...) fusion(f32[1,8,128,256]{3,1,2,0:T(8,128)S(1)} %bitcast.62, ...), kind=kLoop, calls=%fused_computation.50 | loop fusion | flops 6291456 | bytes 9453568 | tf_op jit(solution)/shard_map/convert.6
  65.9 1.1 pad_maximum_fusion
  66.9 1.1 pad_maximum_fusion.1
  68.0 0.5 collective-permute-start.1
  68.5 2.5 %fusion.36 = (bf16[256,256]{1,0:T(8,128)(2,1)S(1)}, bf16[256,256]{1,0:T(8,128)(2,1)S(1)}, bf16[256,256]{1,0:T(8,128)(2,1)S(1)}, bf16[256,256]{1,0:T(8,128)(2,1)S...) fusion(s32[256]{0:T(256)S(1)} %multiply_add_fusion.1), kind=kLoop, calls=%fused_computation.85 | loop fusion | flops 2359296 | bytes 787456 | tf_op jit(solution)/shard_map/convert.15
  71.0 0.1 pad_maximum_fusion.2
  71.2 1.5 %add_convert_fusion.2 = bf16[2,8,128,256]{3,2,1,0:T(8,128)(2,1)S(1)} fusion(bf16[2,8,128,256]{3,2,1,0:T(8,128)(2,1)} %collective-permute-done, f32[]{:T(128)S(6)} %convert_element_type.121, bf16[1,8,128,256]{3,2,1,0:T(8,128)(2,1)S(1)} %get-tuple-element.47, bf16[1,8,128,256]{3,2,1,0:T(8,128)(2,1)S(1)} %get-tuple-element.48), kind=kLoop, calls=%fused_computation.13 | loop fusion | flops 3145728 | bytes 3145732 | tf_op jit(solution)/shard_map/convert_element_type | solution.py:93
  72.9 1.5 %add_convert_fusion.1 = bf16[2,8,128,256]{3,2,1,0:T(8,128)(2,1)S(1)} fusion(bf16[2,8,128,256]{3,2,1,0:T(8,128)(2,1)} %collective-permute-done.1, f32[]{:T(128)S(6)} %convert_element_type.121, bf16[1,8,128,256]{3,2,1,0:T(8,128)(2,1)S(1)} %get-tuple-element.45, bf16[1,8,128,256]{3,2,1,0:T(8,128)(2,1)S(1)} %get-tuple-element.46), kind=kLoop, calls=%fused_computation.12 | loop fusion | flops 3145728 | bytes 3145732 | tf_op jit(solution)/shard_map/convert_element_type | solution.py:93
  74.5 0.3 add_convert_fusion
  75.0 0.8 convolution_multiply_fusion.3
  75.8 0.8 fusion.8
  76.5 0.8 fusion.15
  77.3 1.0 multiply_add_fusion
  78.3 0.7 convolution_convert_fusion.2
  79.1 0.6 collective-permute-start.2
  79.6 0.7 convolution_convert_fusion
  80.5 0.5 add_convert_fusion.5
  81.0 0.8 convolution_convert_fusion.1
  81.8 0.5 collective-permute-start.4
  82.3 0.3 convert_add_fusion.2
  82.7 0.2 fusion.63
  82.8 0.6 collective-permute-done.5
  83.4 0.3 convert_add_fusion
  83.7 0.2 fusion.60
  83.9 1.0 collective-permute-done.4
  84.9 0.3 convert_add_fusion.1
  85.3 0.2 fusion.61
  85.4 1.1 subtract_convert_fusion
  86.7 0.6 copy.68
  87.3 0.4 fusion.2
  87.6 0.9 copy.58
  88.5 3.7 %all-to-all-start.5 = ((bf16[8,128,256]{2,1,0:T(8,128)(2,1)}), bf16[8,128,256]{2,1,0:T(8,128)(2,1)S(1)}, u32[]{:S(2)}, u32[]{:S(2)}) async-start(bf16[8,128,256]{2,1,0:T(8,128)(2,1)} %copy.58), calls=%async_computation.5 | async-start | bytes 1048576 | tf_op jit(solution)/shard_map/all_to_all | solution.py:111
  92.3 0.6 copy.65
  92.9 0.4 fusion
  93.2 0.9 copy.49
  94.1 13.1 %all-to-all-done.5 = bf16[8,128,256]{2,1,0:T(8,128)(2,1)S(1)} async-done(((bf16[8,128,256]{2,1,0:T(8,128)(2,1)}), bf16[8,128,256]{2,1,0:T(8,128)(2,1)S(1)}, u32[]{:S(2)}, u32[]{:S(2)}) %all-to-all-start.5) | async-done | bytes 524320 | tf_op jit(solution)/shard_map/all_to_all | solution.py:111
  107.2 3.6 %all-to-all-start.2 = ((bf16[8,128,256]{2,1,0:T(8,128)(2,1)}), bf16[8,128,256]{2,1,0:T(8,128)(2,1)S(1)}, u32[]{:S(2)}, u32[]{:S(2)}) async-start(bf16[8,128,256]{2,1,0:T(8,128)(2,1)} %copy.49), calls=%async_computation.2 | async-start | bytes 1048576 | tf_op jit(solution)/shard_map/all_to_all | solution.py:111
  111.0 0.6 copy.67
  111.6 0.4 fusion.1
  111.9 0.9 copy.56
  112.8 12.7 %all-to-all-done.2 = bf16[8,128,256]{2,1,0:T(8,128)(2,1)S(1)} async-done(((bf16[8,128,256]{2,1,0:T(8,128)(2,1)}), bf16[8,128,256]{2,1,0:T(8,128)(2,1)S(1)}, u32[]{:S(2)}, u32[]{:S(2)}) %all-to-all-start.2) | async-done | bytes 524320 | tf_op jit(solution)/shard_map/all_to_all | solution.py:111
  125.5 3.6 %all-to-all-start.4 = ((bf16[8,128,256]{2,1,0:T(8,128)(2,1)}), bf16[8,128,256]{2,1,0:T(8,128)(2,1)S(1)}, u32[]{:S(2)}, u32[]{:S(2)}) async-start(bf16[8,128,256]{2,1,0:T(8,128)(2,1)} %copy.56), calls=%async_computation.4 | async-start | bytes 1048576 | tf_op jit(solution)/shard_map/all_to_all | solution.py:111
  129.2 1.0 copy.59
  130.2 1.0 copy.50
  131.2 12.7 %all-to-all-done.4 = bf16[8,128,256]{2,1,0:T(8,128)(2,1)S(1)} async-done(((bf16[8,128,256]{2,1,0:T(8,128)(2,1)}), bf16[8,128,256]{2,1,0:T(8,128)(2,1)S(1)}, u32[]{:S(2)}, u32[]{:S(2)}) %all-to-all-start.4) | async-done | bytes 524320 | tf_op jit(solution)/shard_map/all_to_all | solution.py:111
  143.9 1.0 copy.57
  (21 shorter events, 0.8 us)
Async XLA Ops:
  0.6 9.4 %copy-start = (bf16[256,1024]{1,0:T(8,128)(2,1)S(1)}, bf16[256,1024]{1,0:T(8,128)(2,1)}, u32[]{:S(2)}) copy-start(bf16[256,1024]{1,0:T(8,128)(2,1)} %param.4) | copy-start | bytes 1572868
  0.6 27.5 %copy-start.1 = (bf16[256,1024]{1,0:T(8,128)(2,1)S(1)}, bf16[256,1024]{1,0:T(8,128)(2,1)}, u32[]{:S(2)}) copy-start(bf16[256,1024]{1,0:T(8,128)(2,1)} %param.5) | copy-start | bytes 1572868
  2.8 21.7 %all-to-all-start.1 = ((bf16[8,128,256]{2,1,0:T(8,128)(2,1)}), bf16[8,128,256]{2,1,0:T(8,128)(2,1)S(1)}, u32[]{:S(2)}, u32[]{:S(2)}) async-start(bf16[8,128,256]{2,1,0:T(8,128)(2,1)} %bitcast.7), calls=%async_computation.1 | async-start | bytes 1048576 | tf_op jit(solution)/shard_map/all_to_all | solution.py:90
  24.5 18.3 %all-to-all-start = ((bf16[8,128,256]{2,1,0:T(8,128)(2,1)}), bf16[8,128,256]{2,1,0:T(8,128)(2,1)S(1)}, u32[]{:S(2)}, u32[]{:S(2)}) async-start(bf16[8,128,256]{2,1,0:T(8,128)(2,1)} %bitcast.1), calls=%async_computation | async-start | bytes 1048576 | tf_op jit(solution)/shard_map/all_to_all | solution.py:90
  42.8 18.3 %all-to-all-start.3 = ((bf16[8,128,256]{2,1,0:T(8,128)(2,1)}), bf16[8,128,256]{2,1,0:T(8,128)(2,1)S(1)}, u32[]{:S(2)}, u32[]{:S(2)}) async-start(bf16[8,128,256]{2,1,0:T(8,128)(2,1)} %bitcast.18), calls=%async_computation.3 | async-start | bytes 1048576 | tf_op jit(solution)/shard_map/all_to_all | solution.py:90
  66.9 4.3 %collective-permute-start = (bf16[2,8,128,256]{3,2,1,0:T(8,128)(2,1)}, bf16[2,8,128,256]{3,2,1,0:T(8,128)(2,1)}, u32[]{:S(2)}, u32[]{:S(2)}) collective-permute-start(bf16[2,8,128,256]{3,2,1,0:T(8,128)(2,1)} %pad_maximum_fusion), channel_id=1, source_target_pairs={{0,1},{1,0},{2,3},{3,2},{4,5},{5,4},{6,7},{7,6},{8,9},{9,8},{10,11... | collective-permute-start | bytes 3145736 | tf_op jit(solution)/shard_map/ppermute | solution.py:12
  68.0 4.9 %collective-permute-start.1 = (bf16[2,8,128,256]{3,2,1,0:T(8,128)(2,1)}, bf16[2,8,128,256]{3,2,1,0:T(8,128)(2,1)}, u32[]{:S(2)}, u32[]{:S(2)}) collective-permute-start(bf16[2,8,128,256]{3,2,1,0:T(8,128)(2,1)} %pad_maximum_fusion.1), channel_id=1, source_target_pairs={{0,1},{1,0},{2,3},{3,2},{4,5},{5,4},{6,7},{7,6},{8,9},{9,8},{10,11... | collective-permute-start | bytes 3145736 | tf_op jit(solution)/shard_map/ppermute | solution.py:12
  71.2 3.4 %collective-permute-start.3 = (bf16[2,8,128,256]{3,2,1,0:T(8,128)(2,1)S(1)}, bf16[2,8,128,256]{3,2,1,0:T(8,128)(2,1)S(1)}, u32[]{:S(2)}, u32[]{:S(2)}) collective-permute-start(bf16[2,8,128,256]{3,2,1,0:T(8,128)(2,1)S(1)} %pad_maximum_fusion.2), channel_id=1, source_target_pairs={{0,1},{1,0},{2,3},{3,2},{4,5},{5,4},{6,7},{7,6},{8,9},{9,8},{10,11... | collective-permute-start | bytes 3145736 | tf_op jit(solution)/shard_map/ppermute | solution.py:12
  79.1 3.2 %collective-permute-start.2 = (bf16[1024,512]{1,0:T(8,128)(2,1)S(1)}, bf16[1024,512]{1,0:T(8,128)(2,1)S(1)}, u32[]{:S(2)}, u32[]{:S(2)}) collective-permute-start(bf16[1024,512]{1,0:T(8,128)(2,1)S(1)} %convolution_convert_fusion.2), channel_id=1, source_target_pairs={{0,1},{1,0},{2,3},{3,2},{4,5},{5,4},{6,7},{7,6},{8,9},{9,8},{10,11... | collective-permute-start | bytes 3145736 | tf_op jit(solution)/shard_map/ppermute | solution.py:12
  80.4 3.0 %collective-permute-start.5 = (bf16[1024,512]{1,0:T(8,128)(2,1)S(1)}, bf16[1024,512]{1,0:T(8,128)(2,1)S(1)}, u32[]{:S(2)}, u32[]{:S(2)}) collective-permute-start(bf16[1024,512]{1,0:T(8,128)(2,1)S(1)} %convolution_convert_fusion), channel_id=1, source_target_pairs={{0,1},{1,0},{2,3},{3,2},{4,5},{5,4},{6,7},{7,6},{8,9},{9,8},{10,11... | collective-permute-start | bytes 3145736 | tf_op jit(solution)/shard_map/ppermute | solution.py:12
  81.8 3.1 %collective-permute-start.4 = (bf16[1024,512]{1,0:T(8,128)(2,1)S(1)}, bf16[1024,512]{1,0:T(8,128)(2,1)S(1)}, u32[]{:S(2)}, u32[]{:S(2)}) collective-permute-start(bf16[1024,512]{1,0:T(8,128)(2,1)S(1)} %convolution_convert_fusion.1), channel_id=1, source_target_pairs={{0,1},{1,0},{2,3},{3,2},{4,5},{5,4},{6,7},{7,6},{8,9},{9,8},{10,11... | collective-permute-start | bytes 3145736 | tf_op jit(solution)/shard_map/ppermute | solution.py:12
  88.5 18.7 %all-to-all-start.5 = ((bf16[8,128,256]{2,1,0:T(8,128)(2,1)}), bf16[8,128,256]{2,1,0:T(8,128)(2,1)S(1)}, u32[]{:S(2)}, u32[]{:S(2)}) async-start(bf16[8,128,256]{2,1,0:T(8,128)(2,1)} %copy.58), calls=%async_computation.5 | async-start | bytes 1048576 | tf_op jit(solution)/shard_map/all_to_all | solution.py:111
  107.2 18.3 %all-to-all-start.2 = ((bf16[8,128,256]{2,1,0:T(8,128)(2,1)}), bf16[8,128,256]{2,1,0:T(8,128)(2,1)S(1)}, u32[]{:S(2)}, u32[]{:S(2)}) async-start(bf16[8,128,256]{2,1,0:T(8,128)(2,1)} %copy.49), calls=%async_computation.2 | async-start | bytes 1048576 | tf_op jit(solution)/shard_map/all_to_all | solution.py:111
  125.5 18.3 %all-to-all-start.4 = ((bf16[8,128,256]{2,1,0:T(8,128)(2,1)}), bf16[8,128,256]{2,1,0:T(8,128)(2,1)S(1)}, u32[]{:S(2)}, u32[]{:S(2)}) async-start(bf16[8,128,256]{2,1,0:T(8,128)(2,1)} %copy.56), calls=%async_computation.4 | async-start | bytes 1048576 | tf_op jit(solution)/shard_map/all_to_all | solution.py:111
where the time goes:
time: 146 us; the launch traced here: 145 us
  waiting for transfers between devices  81.3 us (56%)
  starting transfers between devices  27.2 us (19%)
  other arithmetic  15 us (10%)
  local copies, waits for them, and re-layouts  13.6 us (9%)
  matrix products  6.81 us (5%)
    all_to_all x3, waiting for transfers between devices, spectrum(): lax.all_to_all(arranged, 'wide', split_axis=0, concat_axis=0, tiled=True)  41.1 us
    all_to_all x3, waiting for transfers between devices, invert(): lax.all_to_all(arranged, 'wide', split_axis=0, concat_axis=1, tiled=True)  38.5 us
    all_to_all x3, starting transfers between devices, spectrum(): lax.all_to_all(arranged, 'wide', split_axis=0, concat_axis=0, tiled=True)  14.5 us
    all_to_all x3, starting transfers between devices, invert(): lax.all_to_all(arranged, 'wide', split_axis=0, concat_axis=1, tiled=True)  10.9 us
    another operation x5, other arithmetic  6.97 us
    reshape x3, local copies, waits for them, and re-layouts, spectrum(): arranged = jnp.transpose(signal).reshape(span_count, shares, blocksize)  4.13 us
    convert_element_type x3, other arithmetic, spectrum(): (signed * twisted.astype(jnp.float32) + partner.astype(jnp.float32)).asty...  3.43 us
    reshape x3, local copies, waits for them, and re-layouts, invert(): return jnp.transpose(returned.reshape(channels, blocksize))  3 us
  transfers between devices with their start and end apart: 12, of which 8 were waited for; matrix products, arithmetic and copies ran while one was open for 13% of the time, Pallas kernels for 0%

commit v1 on v0

--- a/solution.py
+++ b/solution.py
@@ -2,7 +2,11 @@
 
 import jax
 import jax.numpy as jnp
+import ml_dtypes
+import numpy as np
 from jax import lax
+from jax.experimental import pallas as pl
+from jax.experimental.pallas import tpu as pltpu
 from jax.sharding import PartitionSpec as P
 
 
@@ -134,17 +138,331 @@
     return (outputs, grad_inputs, grad_taps)
 
 
+RADIX = 8
+
+
+def exact_tables(blocksize, seq_len, lanes):
+    j = np.arange(blocksize)
+    mats = []
+    for r in range(2):
+        ang = (j[:, None] * (2 * j[None, :] + r) % (2 * blocksize)).astype(np.float32)
+        ang = ang * np.float32(math.pi / blocksize)
+        cos, sin = np.cos(ang), np.sin(ang)
+        mats.append(np.block([[cos, -sin], [sin, cos]]))
+    inverse = np.stack(mats).astype(ml_dtypes.bfloat16)
+    forward = np.ascontiguousarray(np.transpose(inverse, (0, 2, 1)))
+    k1 = np.arange(1, RADIX // 2 + 1)[:, None, None]
+    n = np.arange(2)[None, :, None]
+    ang = ((n * blocksize + j[None, None, :]) * k1).astype(np.float32)
+    ang = ang * np.float32(2.0 * math.pi / seq_len)
+    shape = (RADIX // 2, 2, blocksize, lanes)
+    cos = np.ascontiguousarray(np.broadcast_to(np.cos(ang)[..., None], shape))
+    sin = np.ascontiguousarray(np.broadcast_to(np.sin(ang)[..., None], shape))
+    return forward, inverse, cos, sin
+
+
+def fused_kernel(
+    x_ref, f_ref, g_ref, fwd_hbm, inv_hbm, cos_hbm, sin_hbm, o0_ref, o1_ref, o2_ref,
+    buf, spec, mix, unf, obuf, fwd, inv, tcos, tsin,
+    send_sem, recv_sem, own_sem, osend_sem, orecv_sem, oown_sem, table_sem,
+):
+    block, lanes = buf.shape[2], buf.shape[3]
+    wide, narrow = lax.axis_index("wide"), lax.axis_index("narrow")
+    half, place = wide // 4, wide % 4
+    mine = wide * 2 + narrow
+    signals = (x_ref, f_ref, g_ref)
+    outs = (o0_ref, o1_ref, o2_ref)
+    root = float(np.float32(ml_dtypes.bfloat16(math.cos(math.pi / 4))))
+
+    def peer(dh, dp, dc):
+        w = (half + dh) % 2 * 4 + (place + dp) % 4
+        return w, (narrow + dc) % 2
+
+    offsets = [(dh, dp, dc) for dh in (1, 0) for dp in (0, 1, 2, 3) for dc in (0, 1)]
+    others = [o for o in offsets if o != (0, 0, 0)]
+
+    def where(w, c):
+        return {"wide": w, "narrow": c}
+
+    def columns(w, c):
+        return pl.ds(pl.multiple_of((w % 4 * 2 + c) * lanes, lanes), lanes)
+
+    tables = [
+        pltpu.make_async_copy(a, b, table_sem.at[i])
+        for i, (a, b) in enumerate(
+            ((cos_hbm, tcos), (sin_hbm, tsin), (fwd_hbm, fwd), (inv_hbm, inv))
+        )
+    ]
+
+    barrier = pltpu.get_barrier_semaphore()
+    for o in others:
+        w, c = peer(*o)
+        pl.semaphore_signal(
+            barrier, inc=1, device_id=where(w, c), device_id_type=pl.DeviceIdType.MESH
+        )
+    pl.semaphore_wait(barrier, len(others))
+
+    def send(s, i):
+        w, c = peer(*others[i])
+        return pltpu.make_async_remote_copy(
+            src_ref=signals[s].at[:, columns(w, c)],
+            dst_ref=buf.at[s, mine],
+            send_sem=send_sem.at[s, i],
+            recv_sem=recv_sem.at[s, mine],
+            device_id=where(w, c),
+            device_id_type=pl.DeviceIdType.MESH,
+        )
+
+    def arrived(s, i):
+        w, c = peer(*others[i])
+        b = w * 2 + c
+        return pltpu.make_async_remote_copy(
+            src_ref=buf.at[s, b],
+            dst_ref=buf.at[s, b],
+            send_sem=send_sem.at[s, i],
+            recv_sem=recv_sem.at[s, b],
+            device_id=where(w, c),
+            device_id_type=pl.DeviceIdType.MESH,
+        )
+
+    def own(s):
+        return pltpu.make_async_copy(
+            signals[s].at[:, columns(wide, narrow)], buf.at[s, mine], own_sem.at[s]
+        )
+
+    def launch(s):
+        for i in range(len(others)):
+            send(s, i).start()
+        own(s).start()
+
+    def collect(s):
+        for i in range(len(others)):
+            arrived(s, i).wait_recv()
+        own(s).wait()
+
+    step = 16
+
+    def forward(s):
+        def tile(t, carry):
+            rows = pl.ds(pl.multiple_of(t * step, step), step)
+            low = pl.ds(pl.multiple_of(t * step + block, step), step)
+            halves = []
+            for n in range(2):
+                a = [buf[s, 2 * i + n, rows, :].astype(jnp.float32) for i in range(RADIX)]
+                e = [a[i] + a[i + 4] for i in range(4)]
+                d = [a[i] - a[i + 4] for i in range(4)]
+                even, odd = e[0] + e[2], e[1] + e[3]
+                minus = root * (d[1] - d[3])
+                plus = root * (d[1] + d[3])
+                raw = [
+                    (d[0] + minus, -(d[2] + plus)),
+                    (e[0] - e[2], e[3] - e[1]),
+                    (d[0] - minus, d[2] - plus),
+                    (even - odd, None),
+                ]
+                got = [(even + odd, None)]
+                for k, (re, im) in enumerate(raw):
+                    cos, sin = tcos[k, n, rows, :], tsin[k, n, rows, :]
+                    if im is None:
+                        got.append((re * cos, -(re * sin)))
+                    else:
+                        got.append((re * cos + im * sin, im * cos - re * sin))
+                halves.append(got)
+            for k in range(RADIX // 2 + 1):
+                cols = slice(k * lanes, (k + 1) * lanes)
+                (r0, i0), (r1, i1) = halves[0][k], halves[1][k]
+                mix[0, rows, cols] = (r0 + r1).astype(jnp.bfloat16)
+                mix[1, rows, cols] = (r0 - r1).astype(jnp.bfloat16)
+                if i0 is not None:
+                    mix[0, low, cols] = (i0 + i1).astype(jnp.bfloat16)
+                    mix[1, low, cols] = (i0 - i1).astype(jnp.bfloat16)
+                else:
+                    mix[0, low, cols] = jnp.zeros_like(r0, jnp.bfloat16)
+                    mix[1, low, cols] = jnp.zeros_like(r0, jnp.bfloat16)
+            return carry
+
+        lax.fori_loop(0, block // step, tile, 0)
+        multiply(fwd, spec.at[s])
+
+    def multiply(table, result):
+        def one(r, carry):
+            width = mix.shape[2]
+            for first in range(0, width, 256):
+                cols = slice(first, min(first + 256, width))
+                result[r, :, cols] = jnp.dot(
+                    table[r], mix[r, :, cols], preferred_element_type=jnp.float32
+                )
+            return carry
+
+        lax.fori_loop(0, 2, one, 0)
+
+    def combine(left, right, conjugate):
+        def tile(t, carry):
+            rows = pl.ds(pl.multiple_of(t * step, step), step)
+            low = pl.ds(pl.multiple_of(t * step + block, step), step)
+            for r in range(2):
+                for k in range(RADIX // 2 + 1):
+                    cols = slice(k * lanes, (k + 1) * lanes)
+                    lr, li = spec[left, r, rows, cols], spec[left, r, low, cols]
+                    rr, ri = spec[right, r, rows, cols], spec[right, r, low, cols]
+                    if conjugate:
+                        re, im = lr * rr + li * ri, lr * ri - li * rr
+                    else:
+                        re, im = lr * rr - li * ri, lr * ri + li * rr
+                    mix[r, rows, cols] = re.astype(jnp.bfloat16)
+                    mix[r, low, cols] = im.astype(jnp.bfloat16)
+            return carry
+
+        lax.fori_loop(0, block // step, tile, 0)
+
+    scale = 2.0 ** -18
+    side = (1 - 2 * half).astype(jnp.float32) * (2.0 * scale)
+
+    def inverse(o, left, right, conjugate):
+        combine(left, right, conjugate)
+        multiply(inv, unf)
+
+        def tile(t, carry):
+            rows = pl.ds(pl.multiple_of(t * step, step), step)
+            low = pl.ds(pl.multiple_of(t * step + block, step), step)
+            for n in range(2):
+                sign = 1 if n == 0 else -1
+                zero = slice(0, lanes)
+                parts = [(unf[0, rows, zero] + sign * unf[1, rows, zero]) * scale]
+                for k in range(RADIX // 2):
+                    cols = slice((k + 1) * lanes, (k + 2) * lanes)
+                    re = unf[0, rows, cols] + sign * unf[1, rows, cols]
+                    im = unf[0, low, cols] + sign * unf[1, low, cols]
+                    cos, sin = tcos[k, n, rows, :], tsin[k, n, rows, :]
+                    mre = re * cos - im * sin
+                    if k == RADIX // 2 - 1:
+                        parts.append(mre * scale)
+                    else:
+                        factor = 2.0 * scale if k == 1 else side
+                        parts.append((mre * factor, (im * cos + re * sin) * factor))
+                a, (r1, i1), (r2, i2), (r3, i3), b = parts
+                top, bottom = a + b, a - b
+                left_, right_ = root * (r1 - r3), root * (i1 + i3)
+                values = (
+                    top + r2 + (r1 + r3),
+                    bottom - i2 + (left_ - right_),
+                    top - r2 + (i3 - i1),
+                    bottom + i2 - (left_ + right_),
+                )
+                for u in range(4):
+                    obuf[o, 2 * u + n, rows, :] = values[u].astype(jnp.bfloat16)
+            return carry
+
+        lax.fori_loop(0, block // step, tile, 0)
+
+    near = [(dp, dc) for dp in range(4) for dc in range(2)][1:]
+
+    def give(o, i):
+        w, c = peer(0, *near[i])
+        return pltpu.make_async_remote_copy(
+            src_ref=obuf.at[o, w % 4 * 2 + c],
+            dst_ref=outs[o].at[:, columns(wide, narrow)],
+            send_sem=osend_sem.at[o, i],
+            recv_sem=orecv_sem.at[o, place * 2 + narrow],
+            device_id=where(w, c),
+            device_id_type=pl.DeviceIdType.MESH,
+        )
+
+    def taken(o, i):
+        w, c = peer(0, *near[i])
+        return pltpu.make_async_remote_copy(
+            src_ref=obuf.at[o, w % 4 * 2 + c],
+            dst_ref=outs[o].at[:, columns(w, c)],
+            send_sem=osend_sem.at[o, i],
+            recv_sem=orecv_sem.at[o, w % 4 * 2 + c],
+            device_id=where(w, c),
+            device_id_type=pl.DeviceIdType.MESH,
+        )
+
+    def keep(o):
+        return pltpu.make_async_copy(
+            obuf.at[o, place * 2 + narrow],
+            outs[o].at[:, columns(wide, narrow)],
+            oown_sem.at[o],
+        )
+
+    def deliver(o):
+        for i in range(len(near)):
+            give(o, i).start()
+        keep(o).start()
+
+    for s in range(3):
+        launch(s)
+    for t in tables:
+        t.start()
+    for t in tables:
+        t.wait()
+    collect(0)
+    forward(0)
+    collect(1)
+    forward(1)
+    inverse(0, 1, 0, False)
+    deliver(0)
+    collect(2)
+    forward(2)
+    inverse(1, 1, 2, True)
+    deliver(1)
+    inverse(2, 0, 2, True)
+    deliver(2)
+    for s in range(3):
+        for i in range(len(others)):
+            send(s, i).wait_send()
+    for o in range(3):
+        for i in range(len(near)):
+            give(o, i).wait_send()
+            taken(o, i).wait_recv()
+        keep(o).wait()
+
+
+def on_device_fused(inputs, filter_taps, grad_out):
+    block, channels = inputs.shape
+    lanes = channels // RADIX
+    tables = exact_tables(block, RADIX * 2 * block, lanes)
+    width = (RADIX // 2 + 1) * lanes
+    out = jax.ShapeDtypeStruct(inputs.shape, jnp.bfloat16)
+    anywhere = pl.BlockSpec(memory_space=pl.ANY)
+    return pl.pallas_call(
+        fused_kernel,
+        out_shape=(out, out, out),
+        in_specs=[anywhere] * 7,
+        out_specs=(anywhere,) * 3,
+        scratch_shapes=[
+            pltpu.VMEM((3, 2 * RADIX, block, lanes), jnp.bfloat16),
+            pltpu.VMEM((3, 2, 2 * block, width), jnp.float32),
+            pltpu.VMEM((2, 2 * block, width), jnp.bfloat16),
+            pltpu.VMEM((2, 2 * block, width), jnp.float32),
+            pltpu.VMEM((3, RADIX, block, lanes), jnp.bfloat16),
+            pltpu.VMEM((2, 2 * block, 2 * block), jnp.bfloat16),
+            pltpu.VMEM((2, 2 * block, 2 * block), jnp.bfloat16),
+            pltpu.VMEM((RADIX // 2, 2, block, lanes), jnp.float32),
+            pltpu.VMEM((RADIX // 2, 2, block, lanes), jnp.float32),
+            pltpu.SemaphoreType.DMA((3, 15)),
+            pltpu.SemaphoreType.DMA((3, 16)),
+            pltpu.SemaphoreType.DMA((3,)),
+            pltpu.SemaphoreType.DMA((3, 7)),
+            pltpu.SemaphoreType.DMA((3, 8)),
+            pltpu.SemaphoreType.DMA((3,)),
+            pltpu.SemaphoreType.DMA((4,)),
+        ],
+        compiler_params=pltpu.CompilerParams(
+            collective_id=0, has_side_effects=True, vmem_limit_bytes=48 * 2**20
+        ),
+    )(inputs, filter_taps, grad_out, *tables)
+
+
 def solution(mesh):
     in_specs = (
         P(("groups", "wide", "narrow"), None),
         P(("wide", "narrow"), None),
         P(("groups", "wide", "narrow"), None),
     )
-    out_specs = (
-        P(("groups", "wide", "narrow"), None),
-        P(("groups", "wide", "narrow"), None),
-        P(("groups", "wide", "narrow"), None),
+    out_specs = (P(("groups", "wide", "narrow"), None),) * 3
+    body = on_device_fused if mesh.shape["wide"] == RADIX else on_device
+    return jax.shard_map(
+        body, mesh=mesh, in_specs=in_specs, out_specs=out_specs, check_vma=False
     )
-    return jax.shard_map(
-        on_device, mesh=mesh, in_specs=in_specs, out_specs=out_specs, check_vma=False
-    )

time: 146 us -> 104 us (0.71)
  Pallas kernels: 0 us -> 94.7 us
  waiting for transfers between devices: 81.3 us -> 0 us
  starting transfers between devices: 27.2 us -> 0 us
  other arithmetic: 15 us -> 0 us
  matrix products: 6.81 us -> 0 us
  local copies, waits for them, and re-layouts: 13.6 us -> 7.95 us
    pallas_call x0 -> x1, Pallas kernels: none -> 94.7 us  [on_device_fused(): pl.pallas_call(fused_kernel, out_shape=(out, out, out), in_specs=[anywher...]
    all_to_all x6 -> x0, waiting for transfers between devices: 79.6 us -> none  [the longest x3 41.1 us: spectrum(): lax.all_to_all(arranged, 'wide', split_axis=0, concat_axis=0, tiled=True)]
    all_to_all x6 -> x0, starting transfers between devices: 25.4 us -> none  [the longest x3 14.5 us: spectrum(): lax.all_to_all(arranged, 'wide', split_axis=0, concat_axis=0, tiled=True)]
    reshape x9 -> x0, local copies, waits for them, and re-layouts: 9.81 us -> none  [the longest x3 4.13 us: spectrum(): arranged = jnp.transpose(signal).reshape(span_count, shares, blocksize)]
    another operation x8 -> x0, other arithmetic: 9.22 us -> none
    dot_general x12 -> x0, matrix products: 6.81 us -> none  [the longest x3 2.28 us: spectrum(): return jnp.dot(joined, forward_mat, preferred_element_type=jnp.float32)]
    unnamed x10 -> x13, local copies, waits for them, and re-layouts: 2.65 us -> 7.95 us
    convert_element_type x3 -> x0, other arithmetic: 3.43 us -> none  [spectrum(): (signed * twisted.astype(jnp.float32) + partner.astype(jnp.float32)).asty...]
  transfers between devices with their start and end apart: 12 -> 0, of which waited for: 8 -> 0; matrix products, arithmetic and copies ran while one was open for 13% -> 0% of each run, Pallas kernels for 0% -> 0%
where the time goes in v1:
time: 104 us; the launch traced here: 103 us
  Pallas kernels  94.7 us (91%)
  local copies, waits for them, and re-layouts  7.95 us (8%)
    pallas_call x1, Pallas kernels, on_device_fused(): pl.pallas_call(fused_kernel, out_shape=(out, out, out), in_specs=[anywher...  94.7 us
    unnamed x13, local copies, waits for them, and re-layouts  7.95 us

profile of v1, /device:TPU:0, one launch (start us, length us, event | category | flops | bytes accessed | tf_op | source)
XLA Modules:
  0.0 103.3 jit_solution(10913823414632773976)
XLA Ops:
  0.6 0.0 copy-start
  0.6 1.2 %copy-done = bf16[2,512,512]{2,1,0:T(8,128)(2,1)S(1)} copy-done((bf16[2,512,512]{2,1,0:T(8,128)(2,1)S(1)}, bf16[2,512,512]{2,1,0:T(8,128)(2,1)}, u32[]{:S(2)}) %copy-start) | copy-done | bytes 1048600
  1.9 0.0 copy-start.1
  1.9 1.2 %copy-done.1 = bf16[2,512,512]{2,1,0:T(8,128)(2,1)S(1)} copy-done((bf16[2,512,512]{2,1,0:T(8,128)(2,1)S(1)}, bf16[2,512,512]{2,1,0:T(8,128)(2,1)}, u32[]{:S(2)}) %copy-start.1) | copy-done | bytes 1048600
  3.1 0.0 copy-start.2
  3.1 1.0 %copy-done.2 = bf16[256,1024]{1,0:T(8,128)(2,1)S(1)} copy-done((bf16[256,1024]{1,0:T(8,128)(2,1)S(1)}, bf16[256,1024]{1,0:T(8,128)(2,1)}, u32[]{:S(2)}) %copy-start.2) | copy-done | bytes 524312
  4.1 0.0 copy-start.3
  4.1 1.0 %copy-done.3 = bf16[256,1024]{1,0:T(8,128)(2,1)S(1)} copy-done((bf16[256,1024]{1,0:T(8,128)(2,1)S(1)}, bf16[256,1024]{1,0:T(8,128)(2,1)}, u32[]{:S(2)}) %copy-start.3) | copy-done | bytes 524312
  5.2 0.0 copy-start.4
  5.2 1.0 %copy-done.4 = bf16[256,1024]{1,0:T(8,128)(2,1)S(1)} copy-done((bf16[256,1024]{1,0:T(8,128)(2,1)S(1)}, bf16[256,1024]{1,0:T(8,128)(2,1)}, u32[]{:S(2)}) %copy-start.4) | copy-done | bytes 524312
  6.2 94.7 %shard_map.94 = (bf16[256,1024]{1,0:T(8,128)(2,1)S(1)}, bf16[256,1024]{1,0:T(8,128)(2,1)S(1)}, bf16[256,1024]{1,0:T(8,128)(2,1)S(1)}) custom-call(bf16[256,1024]{1,0:T(8,128)(2,1)S(1)} %copy-done.2, bf16[256,1024]{1,0:T(8,128)(2,1)S(1)} %copy-done.3, bf16[256,1024]{1,0:T(8,128)(2,1)S(1)} %copy-done.4, bf16[2,512,512]{2,1,0:T(8,128)(2,1)S(1)} %copy-done.1, ...), custom_call_target="tpu_custom_call" | custom-call | tf_op jit(solution)/shard_map/pallas_call | solution.py:429
  100.9 0.8 copy.13
  101.7 0.8 copy.14
  102.5 0.8 copy.15
Async XLA Ops:
  0.6 1.2 %copy-start = (bf16[2,512,512]{2,1,0:T(8,128)(2,1)S(1)}, bf16[2,512,512]{2,1,0:T(8,128)(2,1)}, u32[]{:S(2)}) copy-start(bf16[2,512,512]{2,1,0:T(8,128)(2,1)} %constant.9.clone.inv_hbm) | copy-start | bytes 3145732
  1.9 1.2 %copy-start.1 = (bf16[2,512,512]{2,1,0:T(8,128)(2,1)S(1)}, bf16[2,512,512]{2,1,0:T(8,128)(2,1)}, u32[]{:S(2)}) copy-start(bf16[2,512,512]{2,1,0:T(8,128)(2,1)} %constant.8.clone.fwd_hbm) | copy-start | bytes 3145732
  3.1 1.0 %copy-start.2 = (bf16[256,1024]{1,0:T(8,128)(2,1)S(1)}, bf16[256,1024]{1,0:T(8,128)(2,1)}, u32[]{:S(2)}) copy-start(bf16[256,1024]{1,0:T(8,128)(2,1)} %x_ref.1) | copy-start | bytes 1572868
  4.1 1.0 %copy-start.3 = (bf16[256,1024]{1,0:T(8,128)(2,1)S(1)}, bf16[256,1024]{1,0:T(8,128)(2,1)}, u32[]{:S(2)}) copy-start(bf16[256,1024]{1,0:T(8,128)(2,1)} %f_ref.1) | copy-start | bytes 1572868
  5.2 1.0 %copy-start.4 = (bf16[256,1024]{1,0:T(8,128)(2,1)S(1)}, bf16[256,1024]{1,0:T(8,128)(2,1)}, u32[]{:S(2)}) copy-start(bf16[256,1024]{1,0:T(8,128)(2,1)} %g_ref.1) | copy-start | bytes 1572868

commit v2 on v1

--- a/solution.py
+++ b/solution.py
@@ -165,10 +165,12 @@
     x_ref, f_ref, g_ref, fwd_hbm, inv_hbm, cos_hbm, sin_hbm, o0_ref, o1_ref, o2_ref,
     buf, spec, mix, unf, obuf, fwd, inv, tcos, tsin,
     send_sem, recv_sem, own_sem, osend_sem, orecv_sem, oown_sem, table_sem,
+    relay_send_sem, relay_recv_sem,
 ):
     block, lanes = buf.shape[2], buf.shape[3]
     wide, narrow = lax.axis_index("wide"), lax.axis_index("narrow")
     half, place = wide // 4, wide % 4
+    group = lax.axis_index("groups")
     mine = wide * 2 + narrow
     signals = (x_ref, f_ref, g_ref)
     outs = (o0_ref, o1_ref, o2_ref)
@@ -200,13 +202,24 @@
         pl.semaphore_signal(
             barrier, inc=1, device_id=where(w, c), device_id_type=pl.DeviceIdType.MESH
         )
-    pl.semaphore_wait(barrier, len(others))
+    pl.semaphore_signal(
+        barrier, inc=1, device_id={"groups": 1 - group}, device_id_type=pl.DeviceIdType.MESH
+    )
+    pl.semaphore_wait(barrier, len(others) + 1)
+
+    far = [i for i, o in enumerate(others) if o[0] == 1]
+
+    def share(g):
+        return pl.ds(pl.multiple_of(g * (block // 2), block // 2), block // 2)
+
+    def piece(ref, s, i, g):
+        return ref.at[share(g)] if s == 1 and i in far else ref
 
     def send(s, i):
         w, c = peer(*others[i])
         return pltpu.make_async_remote_copy(
-            src_ref=signals[s].at[:, columns(w, c)],
-            dst_ref=buf.at[s, mine],
+            src_ref=piece(signals[s].at[:, columns(w, c)], s, i, group),
+            dst_ref=piece(buf.at[s, mine], s, i, group),
             send_sem=send_sem.at[s, i],
             recv_sem=recv_sem.at[s, mine],
             device_id=where(w, c),
@@ -217,14 +230,26 @@
         w, c = peer(*others[i])
         b = w * 2 + c
         return pltpu.make_async_remote_copy(
-            src_ref=buf.at[s, b],
-            dst_ref=buf.at[s, b],
+            src_ref=piece(buf.at[s, b], s, i, group),
+            dst_ref=piece(buf.at[s, b], s, i, group),
             send_sem=send_sem.at[s, i],
             recv_sem=recv_sem.at[s, b],
             device_id=where(w, c),
             device_id_type=pl.DeviceIdType.MESH,
         )
 
+    def relay(i, g):
+        w, c = peer(*others[i])
+        rows = piece(buf.at[1, w * 2 + c], 1, i, g)
+        return pltpu.make_async_remote_copy(
+            src_ref=rows,
+            dst_ref=rows,
+            send_sem=relay_send_sem.at[i],
+            recv_sem=relay_recv_sem.at[i],
+            device_id={"groups": 1 - group},
+            device_id_type=pl.DeviceIdType.MESH,
+        )
+
     def own(s):
         return pltpu.make_async_copy(
             signals[s].at[:, columns(wide, narrow)], buf.at[s, mine], own_sem.at[s]
@@ -238,6 +263,11 @@
     def collect(s):
         for i in range(len(others)):
             arrived(s, i).wait_recv()
+            if s == 1 and i in far:
+                relay(i, group).start()
+        if s == 1:
+            for i in far:
+                relay(i, 1 - group).wait_recv()
         own(s).wait()
 
     step = 16
@@ -391,16 +421,17 @@
             give(o, i).start()
         keep(o).start()
 
-    for s in range(3):
-        launch(s)
+    launch(1)
+    launch(0)
+    launch(2)
     for t in tables:
         t.start()
     for t in tables:
         t.wait()
+    collect(1)
+    forward(1)
     collect(0)
     forward(0)
-    collect(1)
-    forward(1)
     inverse(0, 1, 0, False)
     deliver(0)
     collect(2)
@@ -409,6 +440,8 @@
     deliver(1)
     inverse(2, 0, 2, True)
     deliver(2)
+    for i in far:
+        relay(i, group).wait_send()
     for s in range(3):
         for i in range(len(others)):
             send(s, i).wait_send()
@@ -425,7 +458,7 @@
     tables = exact_tables(block, RADIX * 2 * block, lanes)
     width = (RADIX // 2 + 1) * lanes
     out = jax.ShapeDtypeStruct(inputs.shape, jnp.bfloat16)
-    anywhere = pl.BlockSpec(memory_space=pl.ANY)
+    anywhere = pl.BlockSpec(memory_space=pltpu.HBM)
     return pl.pallas_call(
         fused_kernel,
         out_shape=(out, out, out),
@@ -448,6 +481,8 @@
             pltpu.SemaphoreType.DMA((3, 8)),
             pltpu.SemaphoreType.DMA((3,)),
             pltpu.SemaphoreType.DMA((4,)),
+            pltpu.SemaphoreType.DMA((8,)),
+            pltpu.SemaphoreType.DMA((8,)),
         ],
         compiler_params=pltpu.CompilerParams(
             collective_id=0, has_side_effects=True, vmem_limit_bytes=48 * 2**20
@@ -462,7 +497,7 @@
         P(("groups", "wide", "narrow"), None),
     )
     out_specs = (P(("groups", "wide", "narrow"), None),) * 3
-    body = on_device_fused if mesh.shape["wide"] == RADIX else on_device
+    body = on_device_fused if (mesh.shape["wide"], mesh.shape["groups"]) == (RADIX, 2) else on_device
     return jax.shard_map(
         body, mesh=mesh, in_specs=in_specs, out_specs=out_specs, check_vma=False
     )

time: 104 us -> 92.1 us (0.89)
  Pallas kernels: 94.7 us -> 83.1 us
    pallas_call x1, Pallas kernels: 94.7 us -> 83.1 us  [on_device_fused(): pl.pallas_call(fused_kernel, out_shape=(out, out, out), in_specs=[anywher...]
where the time goes in v2:
time: 92.1 us; the launch traced here: 91.7 us
  Pallas kernels  83.1 us (90%)
  local copies, waits for them, and re-layouts  7.95 us (9%)
    pallas_call x1, Pallas kernels, on_device_fused(): pl.pallas_call(fused_kernel, out_shape=(out, out, out), in_specs=[anywher...  83.1 us
    unnamed x13, local copies, waits for them, and re-layouts  7.95 us

profile of v2, /device:TPU:0, one launch (start us, length us, event | category | flops | bytes accessed | tf_op | source)
XLA Modules:
  0.0 91.7 jit_solution(9504268811069298796)
XLA Ops:
  0.6 0.0 copy-start
  0.6 1.2 %copy-done = bf16[2,512,512]{2,1,0:T(8,128)(2,1)S(1)} copy-done((bf16[2,512,512]{2,1,0:T(8,128)(2,1)S(1)}, bf16[2,512,512]{2,1,0:T(8,128)(2,1)}, u32[]{:S(2)}) %copy-start) | copy-done | bytes 1048600
  1.9 0.0 copy-start.1
  1.9 1.2 %copy-done.1 = bf16[2,512,512]{2,1,0:T(8,128)(2,1)S(1)} copy-done((bf16[2,512,512]{2,1,0:T(8,128)(2,1)S(1)}, bf16[2,512,512]{2,1,0:T(8,128)(2,1)}, u32[]{:S(2)}) %copy-start.1) | copy-done | bytes 1048600
  3.1 0.0 copy-start.2
  3.1 1.0 %copy-done.2 = bf16[256,1024]{1,0:T(8,128)(2,1)S(1)} copy-done((bf16[256,1024]{1,0:T(8,128)(2,1)S(1)}, bf16[256,1024]{1,0:T(8,128)(2,1)}, u32[]{:S(2)}) %copy-start.2) | copy-done | bytes 524312
  4.1 0.0 copy-start.3
  4.1 1.0 %copy-done.3 = bf16[256,1024]{1,0:T(8,128)(2,1)S(1)} copy-done((bf16[256,1024]{1,0:T(8,128)(2,1)S(1)}, bf16[256,1024]{1,0:T(8,128)(2,1)}, u32[]{:S(2)}) %copy-start.3) | copy-done | bytes 524312
  5.2 0.0 copy-start.4
  5.2 1.0 %copy-done.4 = bf16[256,1024]{1,0:T(8,128)(2,1)S(1)} copy-done((bf16[256,1024]{1,0:T(8,128)(2,1)S(1)}, bf16[256,1024]{1,0:T(8,128)(2,1)}, u32[]{:S(2)}) %copy-start.4) | copy-done | bytes 524312
  6.2 83.1 %shard_map.94 = (bf16[256,1024]{1,0:T(8,128)(2,1)S(1)}, bf16[256,1024]{1,0:T(8,128)(2,1)S(1)}, bf16[256,1024]{1,0:T(8,128)(2,1)S(1)}) custom-call(bf16[256,1024]{1,0:T(8,128)(2,1)S(1)} %copy-done.2, bf16[256,1024]{1,0:T(8,128)(2,1)S(1)} %copy-done.3, bf16[256,1024]{1,0:T(8,128)(2,1)S(1)} %copy-done.4, bf16[2,512,512]{2,1,0:T(8,128)(2,1)S(1)} %copy-done.1, ...), custom_call_target="tpu_custom_call" | custom-call | tf_op jit(solution)/shard_map/pallas_call | solution.py:462
  89.3 0.8 copy.13
  90.1 0.8 copy.14
  90.9 0.8 copy.15
Async XLA Ops:
  0.6 1.2 %copy-start = (bf16[2,512,512]{2,1,0:T(8,128)(2,1)S(1)}, bf16[2,512,512]{2,1,0:T(8,128)(2,1)}, u32[]{:S(2)}) copy-start(bf16[2,512,512]{2,1,0:T(8,128)(2,1)} %constant.9.clone.inv_hbm) | copy-start | bytes 3145732
  1.9 1.2 %copy-start.1 = (bf16[2,512,512]{2,1,0:T(8,128)(2,1)S(1)}, bf16[2,512,512]{2,1,0:T(8,128)(2,1)}, u32[]{:S(2)}) copy-start(bf16[2,512,512]{2,1,0:T(8,128)(2,1)} %constant.8.clone.fwd_hbm) | copy-start | bytes 3145732
  3.1 1.0 %copy-start.2 = (bf16[256,1024]{1,0:T(8,128)(2,1)S(1)}, bf16[256,1024]{1,0:T(8,128)(2,1)}, u32[]{:S(2)}) copy-start(bf16[256,1024]{1,0:T(8,128)(2,1)} %x_ref.1) | copy-start | bytes 1572868
  4.1 1.0 %copy-start.3 = (bf16[256,1024]{1,0:T(8,128)(2,1)S(1)}, bf16[256,1024]{1,0:T(8,128)(2,1)}, u32[]{:S(2)}) copy-start(bf16[256,1024]{1,0:T(8,128)(2,1)} %f_ref.1) | copy-start | bytes 1572868
  5.2 1.0 %copy-start.4 = (bf16[256,1024]{1,0:T(8,128)(2,1)S(1)}, bf16[256,1024]{1,0:T(8,128)(2,1)}, u32[]{:S(2)}) copy-start(bf16[256,1024]{1,0:T(8,128)(2,1)} %g_ref.1) | copy-start | bytes 1572868

commit v3 on v2

--- a/solution.py
+++ b/solution.py
@@ -256,7 +256,7 @@
         )
 
     def launch(s):
-        for i in range(len(others)):
+        for i in reversed(range(len(others))):
             send(s, i).start()
         own(s).start()
 
@@ -452,6 +452,23 @@
         keep(o).wait()
 
 
+def settle_kernel(a0, a1, a2, o0, o1, o2, held, load_sem, store_sem):
+    pairs = ((a0, o0), (a1, o1), (a2, o2))
+    loads = [
+        pltpu.make_async_copy(a, held.at[i], load_sem.at[i]) for i, (a, _) in enumerate(pairs)
+    ]
+    stores = [
+        pltpu.make_async_copy(held.at[i], o, store_sem.at[i]) for i, (_, o) in enumerate(pairs)
+    ]
+    for load in loads:
+        load.start()
+    for load, store in zip(loads, stores):
+        load.wait()
+        store.start()
+    for store in stores:
+        store.wait()
+
+
 def on_device_fused(inputs, filter_taps, grad_out):
     block, channels = inputs.shape
     lanes = channels // RADIX
@@ -459,7 +476,7 @@
     width = (RADIX // 2 + 1) * lanes
     out = jax.ShapeDtypeStruct(inputs.shape, jnp.bfloat16)
     anywhere = pl.BlockSpec(memory_space=pltpu.HBM)
-    return pl.pallas_call(
+    results = pl.pallas_call(
         fused_kernel,
         out_shape=(out, out, out),
         in_specs=[anywhere] * 7,
@@ -485,9 +502,20 @@
             pltpu.SemaphoreType.DMA((8,)),
         ],
         compiler_params=pltpu.CompilerParams(
-            collective_id=0, has_side_effects=True, vmem_limit_bytes=48 * 2**20
+            collective_id=0, has_side_effects=True, vmem_limit_bytes=60 * 2**20
         ),
     )(inputs, filter_taps, grad_out, *tables)
+    return pl.pallas_call(
+        settle_kernel,
+        out_shape=(out, out, out),
+        in_specs=[anywhere] * 3,
+        out_specs=(anywhere,) * 3,
+        scratch_shapes=[
+            pltpu.VMEM((3,) + inputs.shape, jnp.bfloat16),
+            pltpu.SemaphoreType.DMA((3,)),
+            pltpu.SemaphoreType.DMA((3,)),
+        ],
+    )(*results)
 
 
 def solution(mesh):

time: 92.1 us -> 84.3 us (0.915)
  local copies, waits for them, and re-layouts: 7.95 us -> 0 us
    unnamed x13 -> x0, local copies, waits for them, and re-layouts: 7.95 us -> none
    pallas_call x0 -> x1, Pallas kernels: none -> 2.23 us  [on_device_fused(): pl.pallas_call(settle_kernel, out_shape=(out, out, out), in_specs=[anywhe...]
    pallas_call x1, Pallas kernels: 83.1 us -> 81.3 us  [on_device_fused(): pl.pallas_call(fused_kernel, out_shape=(out, out, out), in_specs=[anywher...]
where the time goes in v3:
time: 84.3 us; the launch traced here: 84.2 us
  Pallas kernels  83.5 us (99%)
    pallas_call x1, Pallas kernels, on_device_fused(): pl.pallas_call(fused_kernel, out_shape=(out, out, out), in_specs=[anywher...  81.3 us
    pallas_call x1, Pallas kernels, on_device_fused(): pl.pallas_call(settle_kernel, out_shape=(out, out, out), in_specs=[anywhe...  2.23 us

profile of v3, /device:TPU:0, one launch (start us, length us, event | category | flops | bytes accessed | tf_op | source)
XLA Modules:
  0.0 84.2 jit_solution(6220158238224281414)
XLA Ops:
  0.6 81.3 %shard_map.94 = (bf16[256,1024]{1,0:T(8,128)(2,1)}, bf16[256,1024]{1,0:T(8,128)(2,1)}, bf16[256,1024]{1,0:T(8,128)(2,1)}) custom-call(bf16[256,1024]{1,0:T(8,128)(2,1)} %x_ref.1, bf16[256,1024]{1,0:T(8,128)(2,1)} %f_ref.1, bf16[256,1024]{1,0:T(8,128)(2,1)} %g_ref.1, bf16[2,512,512]{2,1,0:T(8,128)(2,1)} %constant.8.clone.fwd_hbm, ...), custom_call_target="tpu_custom_call" | custom-call | tf_op jit(solution)/shard_map/pallas_call | solution.py:479
  81.9 2.2 %shard_map.95 = (bf16[256,1024]{1,0:T(8,128)(2,1)}, bf16[256,1024]{1,0:T(8,128)(2,1)}, bf16[256,1024]{1,0:T(8,128)(2,1)}) custom-call(bf16[256,1024]{1,0:T(8,128)(2,1)} %get-tuple-element.6.a0, bf16[256,1024]{1,0:T(8,128)(2,1)} %get-tuple-element.7.a1, bf16[256,1024]{1,0:T(8,128)(2,1)} %get-tuple-element.8.a2), custom_call_target="tpu_custom_call" | custom-call | tf_op jit(solution)/shard_map/pallas_call | solution.py:508

commit v4 on v3

--- a/solution.py
+++ b/solution.py
@@ -261,7 +261,7 @@
         own(s).start()
 
     def collect(s):
-        for i in range(len(others)):
+        for i in reversed(range(len(others))):
             arrived(s, i).wait_recv()
             if s == 1 and i in far:
                 relay(i, group).start()
@@ -417,7 +417,7 @@
         )
 
     def deliver(o):
-        for i in range(len(near)):
+        for i in reversed(range(len(near))):
             give(o, i).start()
         keep(o).start()
 

time: 84.3 us -> 85.6 us (1.015)
  no operation moved by 1% of the time
where the time goes in v4:
time: 85.6 us; the launch traced here: 84.7 us
  Pallas kernels  84 us (98%)
    pallas_call x1, Pallas kernels, on_device_fused(): pl.pallas_call(fused_kernel, out_shape=(out, out, out), in_specs=[anywher...  81.8 us
    pallas_call x1, Pallas kernels, on_device_fused(): pl.pallas_call(settle_kernel, out_shape=(out, out, out), in_specs=[anywhe...  2.23 us

profile of v4, /device:TPU:0, one launch (start us, length us, event | category | flops | bytes accessed | tf_op | source)
XLA Modules:
  0.0 84.7 jit_solution(9287034191127068660)
XLA Ops:
  0.6 81.8 %shard_map.94 = (bf16[256,1024]{1,0:T(8,128)(2,1)}, bf16[256,1024]{1,0:T(8,128)(2,1)}, bf16[256,1024]{1,0:T(8,128)(2,1)}) custom-call(bf16[256,1024]{1,0:T(8,128)(2,1)} %x_ref.1, bf16[256,1024]{1,0:T(8,128)(2,1)} %f_ref.1, bf16[256,1024]{1,0:T(8,128)(2,1)} %g_ref.1, bf16[2,512,512]{2,1,0:T(8,128)(2,1)} %constant.8.clone.fwd_hbm, ...), custom_call_target="tpu_custom_call" | custom-call | tf_op jit(solution)/shard_map/pallas_call | solution.py:479
  82.4 2.2 %shard_map.95 = (bf16[256,1024]{1,0:T(8,128)(2,1)}, bf16[256,1024]{1,0:T(8,128)(2,1)}, bf16[256,1024]{1,0:T(8,128)(2,1)}) custom-call(bf16[256,1024]{1,0:T(8,128)(2,1)} %get-tuple-element.6.a0, bf16[256,1024]{1,0:T(8,128)(2,1)} %get-tuple-element.7.a1, bf16[256,1024]{1,0:T(8,128)(2,1)} %get-tuple-element.8.a2), custom_call_target="tpu_custom_call" | custom-call | tf_op jit(solution)/shard_map/pallas_call | solution.py:508
